TPU v7x, 32 devices: a whole 2x2x4 slice. The times are simulated.
32 devices in a mesh: grp: 2 (over y), pair: 4 (over z), occ: 2 (over x), rep: 2 (over core).
Axes of the slice: x: 2, y: 2, z: 4, core: 2. Of those that a mesh axis runs over, the one named last changes fastest.
Arguments:
- pair_tiles: bfloat16 [192, 16, 4096], P(('grp', 'pair'), ('occ', 'rep')), parts along dimension 0, may hold values from -6 to 6
- block_list: int32 [192, 2], P(('grp', 'pair')), parts along dimension 0, may hold values from 0 to 79, as said below
- owner_blocks: int32 [8, 4], P('grp'), parts along dimension 0, may hold values from 0 to 15, as said below
- coulomb_metric: bfloat16 [2048, 1024], P(('grp', 'pair'), ('occ', 'rep')), parts along dimension 0, may hold values from -0.5 to 0.5
Outputs:
- contracted: bfloat16 [192, 16, 4096], P(('grp', 'pair'), ('occ', 'rep')), parts along dimension 0
- pol_blocks: float32 [192, 4096], P(('grp', 'pair', 'occ', 'rep')), parts along dimension 0
There are 2 independent parts, one for each index of `grp`. A program takes and returns all parts, laid end to end along the dimension named above; each array names one. Nothing has to cross between parts.
Inputs may be any that keep to these rules, and one draw needn't show every extreme that they name: owner_blocks holds every auxiliary block once. `block_list`: column 0 is a nu-block: tiles on index j of pair have nu-blocks in j * 20 to (j + 1) * 20 - 1. Column 1 is an auxiliary block. Tiles come in pairs with one nu-block and two different auxiliary blocks; no other tile has that nu-block. At most 12 tiles of one index of pair have auxiliary blocks of one owner, and one owner gets exactly 12 from every index of pair.
All inputs are finite; a program needn't handle non-finite values.
Results may differ from a plain program's by a relative error of at most 0.0075.
Values may be sent and summed in bfloat16 or wider, within the bound.
A program may use at most 64 MiB of HBM per device.

v0:
```python
import jax
import jax.numpy as jnp
from jax import lax
from jax.sharding import PartitionSpec as P

BLK = 64
PBD = 4


def pick_blocks(strip_blocks, block_meta):
    self_block = strip_blocks[block_meta[:, 0], block_meta[:, 1]]
    other_block = strip_blocks[block_meta[:, 0], block_meta[:, 2]]
    return jnp.stack([self_block, other_block], axis=1)


def per_device(pair_tiles, block_list, owner_blocks, coulomb_metric):
    slot_count = pair_tiles.shape[0]
    occ_rows = pair_tiles.shape[1]
    row_count = occ_rows * BLK
    pair_count = lax.axis_size("pair")
    capacity = max(2, 2 * slot_count // pair_count)
    buffer_slots = pair_count * capacity
    nu_block = block_list[:, 0]
    aux_block = block_list[:, 1]
    matched = (owner_blocks[None, :, :] == aux_block[:, None, None]).astype(jnp.int32)
    owner_index = jnp.sum(
        matched * jnp.arange(pair_count, dtype=jnp.int32)[None, :, None], axis=(1, 2)
    )
    local_index = jnp.sum(matched * jnp.arange(PBD, dtype=jnp.int32)[None, None, :], axis=(1, 2))
    position = jnp.arange(slot_count, dtype=jnp.int32)
    same_nu = (
        (nu_block[:, None] == nu_block[None, :]) & (position[:, None] != position[None, :])
    ).astype(jnp.int32)
    partner_index = jnp.sum(same_nu * position[None, :], axis=1)
    partner_aux = jnp.sum(same_nu * aux_block[None, :], axis=1)
    earlier = (owner_index[:, None] == owner_index[None, :]) & (
        position[None, :] < position[:, None]
    )
    slot_rank = jnp.sum(earlier.astype(jnp.int32), axis=1)
    slot_place = owner_index * capacity + slot_rank
    flat_tiles = pair_tiles.reshape(slot_count, row_count, BLK)
    live_flag = jnp.ones((slot_count,), jnp.int32)
    block_meta = jnp.stack([local_index, aux_block, partner_aux, live_flag], axis=1)
    send_meta = jnp.zeros((buffer_slots, 4), jnp.int32).at[slot_place].set(block_meta)
    strip = lax.all_gather(coulomb_metric, ("occ", "rep"), axis=1, tiled=True)
    block_count = strip.shape[1] // BLK
    strip_blocks = strip.reshape(PBD, BLK, block_count, BLK).transpose(0, 2, 1, 3)
    send_tiles = (
        jnp.zeros((buffer_slots, row_count, BLK), jnp.bfloat16).at[slot_place].set(flat_tiles)
    )
    got_tiles, got_meta = (
        lax.all_to_all(send_tiles, "pair", split_axis=0, concat_axis=0, tiled=True),
        lax.all_to_all(send_meta, "pair", split_axis=0, concat_axis=0, tiled=True),
    )
    blocks = pick_blocks(strip_blocks, got_meta)
    products = jnp.einsum(
        "trc,tkcd->tkrd", got_tiles, blocks, preferred_element_type=jnp.float32
    ).astype(jnp.bfloat16)
    returned = lax.all_to_all(products, "pair", split_axis=0, concat_axis=0, tiled=True)
    own_products = returned[slot_place]
    total = own_products[:, 0].astype(jnp.float32) + own_products[partner_index, 1].astype(
        jnp.float32
    )
    rounded = total.astype(jnp.bfloat16)
    contracted = rounded.reshape(slot_count, occ_rows, BLK * BLK)
    pol_terms = jnp.einsum(
        "srp,srq->spq", rounded, rounded, preferred_element_type=jnp.float32
    ).reshape(slot_count, BLK * BLK)
    pol_blocks = lax.psum_scatter(
        pol_terms.astype(jnp.bfloat16), ("occ", "rep"), scatter_dimension=0, tiled=True
    ).astype(jnp.float32)
    return (contracted, pol_blocks)


def solution(mesh):
    placed = (
        P(("grp", "pair"), ("occ", "rep"), None),
        P(("grp", "pair"), None),
        P("grp", None),
        P(("grp", "pair"), ("occ", "rep")),
    )
    return jax.shard_map(
        per_device,
        mesh=mesh,
        in_specs=placed,
        out_specs=(
            P(("grp", "pair"), ("occ", "rep"), None),
            P(("grp", "pair", "occ", "rep"), None),
        ),
        check_vma=False,
    )
```

profile of v0, /device:TPU:1, one launch (start us, length us, event | category | flops | bytes accessed | tf_op | source)
XLA Modules:
  0.0 167.4 jit_solution(13021776031701170294)
XLA Ops:
  0.6 0.8 fusion.30
  1.6 0.8 fusion.13
  2.8 0.7 scatter_custom_fusion
  3.6 0.6 copy.44
  4.2 5.4 %all-to-all-start = ((s32[4,12,4]{1,2,0:T(4,128)}), s32[4,12,4]{1,2,0:T(4,128)S(1)}, u32[]{:S(2)}, u32[]{:S(2)}) async-start(s32[4,12,4]{1,2,0:T(4,128)} %copy.44), calls=%async_computation | async-start | bytes 16384 | tf_op jit(solution)/shard_map/all_to_all | solution.py:53
  9.6 2.7 %reshape.111 = bf16[24,256,64]{2,1,0:T(8,128)(2,1)S(1)} reshape(bf16[24,4,4096]{2,1,0:T(4,128)(2,1)} %param.4) | data formatting | bytes 1572864 | tf_op jit(solution)/shard_map/reshape | solution.py:41
  12.3 0.7 copy.48
  13.0 1.3 broadcast_in_dim.5
  14.3 4.6 %scatter_fusion = bf16[48,256,64]{1,2,0:T(8,128)(2,1)} fusion(bf16[48,256,64]{1,2,0:T(8,128)(2,1)} %broadcast_in_dim.5, s32[24]{0:T(128)S(1)} %fusion.14, bf16[24,256,64]{1,2,0:T(8,128)(2,1)S(1)} %copy.48), kind=kCustom, calls=%fused_computation.5 | custom fusion | bytes 2359392 | tf_op jit(solution)/shard_map/scatter | solution.py:49
  18.9 4.7 %all-to-all-start.1 = ((bf16[48,256,64]{1,2,0:T(8,128)(2,1)}), bf16[48,256,64]{1,2,0:T(8,128)(2,1)S(1)}, u32[]{:S(2)}, u32[]{:S(2)}) async-start(bf16[48,256,64]{1,2,0:T(8,128)(2,1)} %scatter_fusion), calls=%async_computation.1 | async-start | bytes 3145728 | tf_op jit(solution)/shard_map/all_to_all | solution.py:52
  23.6 8.5 %all_gather.3 = bf16[256,1024]{1,0:T(8,128)(2,1)S(1)} all-gather(bf16[256,256]{1,0:T(8,128)(2,1)S(1)} %copy-done.1), channel_id=1, replica_groups=mesh['grp'=2,'pair'=4,'occ'=2,'rep'=2] {'occ','rep'}, dimensions={1}, use_global_device_ids=true | all-gather | bytes 655360 | tf_op jit(solution)/shard_map/all_gather | solution.py:45
  32.1 1.6 reshape.68
  33.7 1.5 copy.53
  35.3 1.8 %gather_fusion.1 = bf16[48,64,64]{2,1,0:T(8,128)(2,1)} fusion(bf16[4,16,64,64]{3,2,1,0:T(8,128)(2,1)S(1)} %bitcast.49, s32[48]{0:T(128)S(1)} %get-tuple-element.7), kind=kCustom, calls=%fused_computation.1 | custom fusion | bytes 786816 | tf_op jit(solution)/shard_map/gather | solution.py:12
  37.1 0.9 gather_fusion
  38.3 1.5 copy.47
  39.8 20.2 %all-to-all-done.1 = bf16[48,256,64]{1,2,0:T(8,128)(2,1)S(1)} async-done(((bf16[48,256,64]{1,2,0:T(8,128)(2,1)}), bf16[48,256,64]{1,2,0:T(8,128)(2,1)S(1)}, u32[]{:S(2)}, u32[]{:S(2)}) %all-to-all-start.1) | async-done | bytes 1572896 | tf_op jit(solution)/shard_map/all_to_all | solution.py:52
  60.0 2.7 %convert_bitcast_fusion = bf16[48,2,256,64]{2,3,1,0:T(8,128)(2,1)} fusion(bf16[48,1,64,64]{2,3,1,0:T(8,128)(2,1)S(1)} %bitcast.52, bf16[48,1,64,64]{2,3,1,0:T(8,128)(2,1)S(1)} %bitcast.51, bf16[48,256,64]{1,2,0:T(8,128)(2,1)S(1)} %all-to-all-done.1), kind=kOutput, calls=%fused_computation.6 | convolution fusion | flops 203292672 | bytes 5505024 | tf_op jit(solution)/shard_map/trc,tkcd->tkrd/dot_general | solution.py:56
  62.7 4.8 %all-to-all-start.2 = ((bf16[48,2,256,64]{2,3,1,0:T(8,128)(2,1)}), bf16[48,2,256,64]{2,3,1,0:T(8,128)(2,1)}, u32[]{:S(2)}, u32[]{:S(2)}) async-start(bf16[48,2,256,64]{2,3,1,0:T(8,128)(2,1)} %convert_bitcast_fusion), calls=%async_computation.2 | async-start | bytes 6291456 | tf_op jit(solution)/shard_map/all_to_all | solution.py:59
  67.5 0.6 dynamic-slice.4
  68.7 68.9 %all-to-all-done.2 = bf16[48,2,256,64]{2,3,1,0:T(8,128)(2,1)} async-done(((bf16[48,2,256,64]{2,3,1,0:T(8,128)(2,1)}), bf16[48,2,256,64]{2,3,1,0:T(8,128)(2,1)}, u32[]{:S(2)}, u32[]{:S(2)}) %all-to-all-start.2) | async-done | bytes 3145760 | tf_op jit(solution)/shard_map/all_to_all | solution.py:59
  137.7 2.5 %gather_fusion.2 = bf16[24,2,256,64]{2,3,1,0:T(8,128)(2,1)S(1)} fusion(bf16[48,2,256,64]{2,3,1,0:T(8,128)(2,1)} %all-to-all-done.2, s32[1024]{0:T(1024)S(1)} %pad_clamp_fusion), kind=kCustom, calls=%fused_computation.2 | custom fusion | bytes 3145824 | tf_op jit(solution)/shard_map/gather | solution.py:60
  140.2 1.3 slice_convert_fusion
  141.5 0.7 gather_fusion.3
  142.6 2.0 %copy.50 = f32[24,256,64]{2,1,0:T(8,128)} copy(bf16[24,256,64]{1,2,0:T(8,128)(2,1)S(1)} %gather_fusion.3) | data formatting | bytes 2359296 | tf_op jit(solution)/shard_map/convert_element_type | solution.py:61
  145.0 8.3 %fusion = bf16[8,4096]{1,0:T(8,128)(2,1)S(1)} fusion(bf16[24,4096]{1,0:T(8,128)(2,1)S(1)} %convert_element_type.60), kind=kCustom, calls=%all-reduce-scatter | all-reduce-scatter fusion | flops 131073 | bytes 262656
  153.3 4.3 %collective-permute-start = (bf16[6,4096]{1,0:T(8,128)(2,1)S(1)}, bf16[6,4096]{1,0:T(8,128)(2,1)S(1)}, u32[]{:S(2)}, u32[]{:S(2)}) collective-permute-start(bf16[6,4096]{1,0:T(8,128)(2,1)S(1)} %slice.34), channel_id=1, source_target_pairs={{0,1},{1,2},{2,3},{4,5},{5,6},{6,7},{8,9},{9,10},{10,11},{12,13},{... | collective-permute-start | bytes 147464
  157.6 2.1 %copy.49 = f32[24,1,256,64]{3,2,0,1:T(8,128)S(1)} copy(f32[24,1,256,64]{2,3,1,0:T(8,128)} %slice_convert_fusion) | data formatting | bytes 3145728 | tf_op jit(solution)/shard_map/convert_element_type | solution.py:61
  159.7 2.2 %reshape.70 = f32[24,4,4096]{2,1,0:T(4,128)} reshape(f32[24,1,256,64]{3,2,0,1:T(8,128)S(1)} %copy.49) | data formatting | bytes 3145728 | tf_op jit(solution)/shard_map/convert_element_type | solution.py:61
  161.9 3.2 %reshape.71 = f32[24,4,4096]{2,1,0:T(4,128)S(1)} reshape(f32[24,256,64]{2,1,0:T(8,128)} %copy.50) | data formatting | bytes 3145728 | tf_op jit(solution)/shard_map/convert_element_type | solution.py:61
  165.1 1.3 add_convert_fusion
  166.7 0.7 dynamic-slice_convert_fusion
  (26 shorter events, 2.2 us)
Async XLA Ops:
  4.2 14.7 %all-to-all-start = ((s32[4,12,4]{1,2,0:T(4,128)}), s32[4,12,4]{1,2,0:T(4,128)S(1)}, u32[]{:S(2)}, u32[]{:S(2)}) async-start(s32[4,12,4]{1,2,0:T(4,128)} %copy.44), calls=%async_computation | async-start | bytes 16384 | tf_op jit(solution)/shard_map/all_to_all | solution.py:53
  18.9 4.7 %copy-start.1 = (bf16[256,256]{1,0:T(8,128)(2,1)S(1)}, bf16[256,256]{1,0:T(8,128)(2,1)}, u32[]{:S(2)}) copy-start(bf16[256,256]{1,0:T(8,128)(2,1)} %param.7) | copy-start | bytes 393220
  18.9 41.1 %all-to-all-start.1 = ((bf16[48,256,64]{1,2,0:T(8,128)(2,1)}), bf16[48,256,64]{1,2,0:T(8,128)(2,1)S(1)}, u32[]{:S(2)}, u32[]{:S(2)}) async-start(bf16[48,256,64]{1,2,0:T(8,128)(2,1)} %scatter_fusion), calls=%async_computation.1 | async-start | bytes 3145728 | tf_op jit(solution)/shard_map/all_to_all | solution.py:52
  62.7 4.8 %copy-start.2 = (u32[32]{0:T(128)S(1)}, u32[32]{0:T(128)}, u32[]{:S(2)}) copy-start(u32[32]{0:T(128)} %constant.68) | copy-start | bytes 388
  62.7 75.0 %all-to-all-start.2 = ((bf16[48,2,256,64]{2,3,1,0:T(8,128)(2,1)}), bf16[48,2,256,64]{2,3,1,0:T(8,128)(2,1)}, u32[]{:S(2)}, u32[]{:S(2)}) async-start(bf16[48,2,256,64]{2,3,1,0:T(8,128)(2,1)} %convert_bitcast_fusion), calls=%async_computation.2 | async-start | bytes 6291456 | tf_op jit(solution)/shard_map/all_to_all | solution.py:59
  153.3 13.1 %collective-permute-start = (bf16[6,4096]{1,0:T(8,128)(2,1)S(1)}, bf16[6,4096]{1,0:T(8,128)(2,1)S(1)}, u32[]{:S(2)}, u32[]{:S(2)}) collective-permute-start(bf16[6,4096]{1,0:T(8,128)(2,1)S(1)} %slice.34), channel_id=1, source_target_pairs={{0,1},{1,2},{2,3},{4,5},{5,6},{6,7},{8,9},{9,10},{10,11},{12,13},{... | collective-permute-start | bytes 147464
  161.9 3.2 %copy-start = (f32[24,4,4096]{2,1,0:T(4,128)S(1)}, f32[24,4,4096]{2,1,0:T(4,128)}, u32[]{:S(2)}) copy-start(f32[24,4,4096]{2,1,0:T(4,128)} %reshape.70) | copy-start | bytes 4718596
where the time goes:
time: 168 us; the launch traced here: 167 us
  waiting for transfers between devices  89.1 us (53%)
  local copies, waits for them, and re-layouts  33.2 us (20%)
  starting transfers between devices  19.1 us (11%)
  blocking collectives  16.8 us (10%)
  other arithmetic  4.58 us (3%)
  matrix products  3.02 us (2%)
    all_to_all x1, waiting for transfers between devices, per_device(): lax.all_to_all(products, 'pair', split_axis=0, concat_axis=0, tiled=True)  68.9 us
    all_to_all x1, waiting for transfers between devices, per_device(): lax.all_to_all(send_tiles, 'pair', split_axis=0, concat_axis=0, tiled=True)  20.2 us
    all_gather x1, blocking collectives, per_device(): strip = lax.all_gather(coulomb_metric, ('occ', 'rep'), axis=1, tiled=True)  8.51 us
    unnamed x1, blocking collectives  8.33 us
    all_to_all x1, starting transfers between devices, per_device(): lax.all_to_all(send_meta, 'pair', split_axis=0, concat_axis=0, tiled=True)  5.42 us
    convert_element_type x2, local copies, waits for them, and re-layouts, per_device(): own_products[partner_index, 1].astype(jnp.float32)  5.22 us
    all_to_all x1, starting transfers between devices, per_device(): lax.all_to_all(products, 'pair', split_axis=0, concat_axis=0, tiled=True)  4.77 us
    all_to_all x1, starting transfers between devices, per_device(): lax.all_to_all(send_tiles, 'pair', split_axis=0, concat_axis=0, tiled=True)  4.66 us
  transfers between devices with their start and end apart: 4, of which 2 were waited for; matrix products, arithmetic and copies ran while one was open for 16% of the time, Pallas kernels for 0%

commit v1 on v0

v1 whole, which is shorter than its diff:
```python
import functools

import jax
import jax.numpy as jnp
from jax import lax
from jax.experimental import pallas as pl
from jax.experimental.pallas import tpu as pltpu
from jax.sharding import PartitionSpec as P

BLK = 64
PBD = 4
LANES = 128
MESH = pl.DeviceIdType.MESH
GATHER_LIMIT = 8 << 20


def block_exchange(pair_tiles, block_list, owner_blocks, coulomb_metric):
    slots, occ_rows = pair_tiles.shape[:2]
    rows = occ_rows * BLK
    pairs = lax.axis_size("pair")
    me = lax.axis_index("pair")
    capacity = max(2, 2 * slots // pairs)
    strip = lax.all_gather(coulomb_metric, ("occ", "rep"), axis=1, tiled=True)
    lists = lax.all_gather(block_list, "pair", axis=0, tiled=False)
    nu, aux = lists[:, :, 0], lists[:, :, 1]
    matched = (owner_blocks[None, None] == aux[:, :, None, None]).astype(jnp.int32)
    owner = jnp.sum(matched * jnp.arange(pairs, dtype=jnp.int32)[:, None], axis=(2, 3))
    local = jnp.sum(matched * jnp.arange(PBD, dtype=jnp.int32)[None, :], axis=(2, 3))
    position = jnp.arange(slots, dtype=jnp.int32)
    same_nu = (
        (nu[:, :, None] == nu[:, None, :]) & (position[:, None] != position[None, :])
    ).astype(jnp.int32)
    partner = jnp.sum(same_nu * position, axis=2)
    partner_aux = jnp.sum(same_nu * aux[:, None, :], axis=2)
    earlier = (owner[:, :, None] == owner[:, None, :]) & (position[None, :] < position[:, None])
    rank = jnp.sum(earlier.astype(jnp.int32), axis=2)
    chosen = (
        (owner == me)[:, None, :] & (rank[:, None, :] == jnp.arange(capacity)[None, :, None])
    ).astype(jnp.int32)
    send_local = jnp.sum(chosen * local[:, None, :], axis=2)
    send_aux = jnp.sum(chosen * aux[:, None, :], axis=2)
    send_partner = jnp.sum(chosen * partner_aux[:, None, :], axis=2)
    blocks = strip.reshape(PBD, BLK, -1, BLK).transpose(0, 2, 1, 3)
    send = jnp.stack([blocks[send_local, send_aux], blocks[send_local, send_partner]], axis=2)
    got = lax.all_to_all(send, "pair", split_axis=0, concat_axis=0, tiled=True)
    got = got.reshape(pairs * capacity, 2, BLK, BLK)
    mine = got[owner[me] * capacity + rank[me]]
    tiles = pair_tiles.reshape(slots, rows, BLK)
    products = jnp.einsum(
        "trc,tkcd->tkrd", tiles, mine, preferred_element_type=jnp.float32
    ).astype(jnp.bfloat16)
    total = products[:, 0].astype(jnp.float32) + products[partner[me], 1].astype(jnp.float32)
    rounded = total.astype(jnp.bfloat16)
    pol = jnp.einsum("srp,srq->spq", rounded, rounded, preferred_element_type=jnp.float32)
    pol = pol.reshape(slots, BLK * BLK).astype(jnp.bfloat16)
    pol = lax.psum_scatter(pol, ("occ", "rep"), scatter_dimension=0, tiled=True)
    return rounded.reshape(slots, occ_rows, BLK * BLK), pol.astype(jnp.float32)


def fused_kernel(
    pairs,
    n_occ,
    slots,
    lists,
    owners,
    tiles_hbm,
    metric_hbm,
    out_hbm,
    pol_ref,
    held,
    tiles,
    out,
    pol_send,
    pol_got,
    spread,
    place,
    mate,
    local_sem,
    tiles_sem,
    out_sem,
    right_send,
    left_send,
    line_got,
    x_send,
    x_got,
    core_send,
    core_got,
    pol_out_sem,
    pol_in_sem,
):
    j = lax.axis_index("pair")
    occ = lax.axis_index("occ")
    rep = lax.axis_index("rep")
    plane = 2 * n_occ
    me = occ * 2 + rep
    halves = held.shape[3]
    per_dev = slots // plane
    packs = per_dev // 2
    other_x = {"occ": 1 - occ}
    other_core = {"rep": 1 - rep}
    other_both = {"occ": 1 - occ, "rep": 1 - rep}

    load_metric = [
        pltpu.make_async_copy(
            metric_hbm.at[k * BLK : (k + 1) * BLK, h * LANES : (h + 1) * LANES],
            held.at[j, me, k, h],
            local_sem.at[k, h],
        )
        for k in range(PBD)
        for h in range(halves)
    ]
    for copy in load_metric:
        copy.start()
    load_tiles = pltpu.make_async_copy(tiles_hbm, tiles, tiles_sem)
    load_tiles.start()

    barrier = pltpu.get_barrier_semaphore()

    def greet(device):
        pl.semaphore_signal(barrier, inc=1, device_id=device, device_id_type=MESH)

    greet(other_x)
    greet(other_core)
    greet(other_both)

    @pl.when(j > 0)
    def _():
        greet({"pair": j - 1})

    @pl.when(j < pairs - 1)
    def _():
        greet({"pair": j + 1})

    inner = (j > 0) & (j < pairs - 1)

    @pl.when(inner)
    def _():
        pl.semaphore_wait(barrier, 5)

    @pl.when(jnp.logical_not(inner))
    def _():
        pl.semaphore_wait(barrier, 4)

    for copy in load_metric:
        copy.wait()

    def right(o):
        return pltpu.make_async_remote_copy(
            held.at[o, me], held.at[o, me], right_send.at[o], line_got.at[o], {"pair": j + 1}, MESH
        )

    def left(o):
        return pltpu.make_async_remote_copy(
            held.at[o, me], held.at[o, me], left_send.at[o], line_got.at[o], {"pair": j - 1}, MESH
        )

    def across(o):
        return pltpu.make_async_remote_copy(
            held.at[o, me], held.at[o, me], x_send.at[o], x_got.at[o], other_x, MESH
        )

    def arrived_x(o):
        col = (1 - occ) * 2 + rep
        return pltpu.make_async_remote_copy(
            held.at[o, col], held.at[o, col], x_send.at[o], x_got.at[o], other_x, MESH
        )

    def to_core(o, which):
        col = which * 2 + rep
        return pltpu.make_async_remote_copy(
            held.at[o, col],
            held.at[o, col],
            core_send.at[o, which],
            core_got.at[o, which],
            other_core,
            MESH,
        )

    def from_core(o, which):
        col = which * 2 + 1 - rep
        return pltpu.make_async_remote_copy(
            held.at[o, col],
            held.at[o, col],
            core_send.at[o, which],
            core_got.at[o, which],
            other_core,
            MESH,
        )

    @pl.when(j < pairs - 1)
    def _():
        right(j).start()

    @pl.when(j > 0)
    def _():
        left(j).start()

    across(j).start()
    to_core(j, occ).start()

    def find(s, carry):
        aux = lists[1, s]
        nu = lists[0, s]
        where_ = jnp.int32(0)
        for k in range(pairs * PBD):
            where_ = jnp.where(owners[k // PBD, k % PBD] == aux, k, where_)
        place[s] = where_
        other = jnp.int32(0)
        for t in range(slots):
            other = jnp.where((lists[0, t] == nu) & (s != t), t, other)
        mate[s] = other
        return carry

    lax.fori_loop(0, slots, find, 0)

    def from_x(o):
        arrived_x(o).wait_recv()
        to_core(o, 1 - occ).start()

    from_x_levels = [[j]]
    for d in range(1, pairs):
        lo, hi = j - d, j + d

        @pl.when(lo >= 0)
        def _(lo=lo):
            right(lo).wait_recv()

            @pl.when(j < pairs - 1)
            def _():
                right(lo).start()

            across(lo).start()
            to_core(lo, occ).start()

        @pl.when(hi < pairs)
        def _(hi=hi):
            left(hi).wait_recv()

            @pl.when(j > 0)
            def _():
                left(hi).start()

            across(hi).start()
            to_core(hi, occ).start()

        if d == 1:
            from_x(j)
        else:
            for o in (j - d + 1, j + d - 1):

                @pl.when((o >= 0) & (o < pairs))
                def _(o=o):
                    from_x(o)

    for o in (j - pairs + 1, j + pairs - 1):

        @pl.when((o >= 0) & (o < pairs))
        def _(o=o):
            from_x(o)

    load_tiles.wait()

    def settle(o, carry):
        from_core(o, 0).wait_recv()
        from_core(o, 1).wait_recv()
        to_core(o, 0).wait_send()
        to_core(o, 1).wait_send()
        across(o).wait_send()

        @pl.when((o <= j) & (j < pairs - 1))
        def _():
            right(o).wait_send()

        @pl.when((o >= j) & (j > 0))
        def _():
            left(o).wait_send()

        return carry

    lax.fori_loop(0, pairs, settle, 0)

    lane = lax.broadcasted_iota(jnp.int32, (BLK, LANES), 1)
    low = lane < BLK

    def weights(row, col):
        half = col // 2
        x = held[row // PBD, half // halves, row % PBD, half % halves].astype(jnp.float32)
        turned = pltpu.roll(x, BLK, 1)
        even = jnp.full((BLK, LANES), col % 2, jnp.int32) == 0
        first = jnp.where(low, jnp.where(even, x, turned), 0.0)
        second = jnp.where(low, 0.0, jnp.where(even, turned, x))
        return jnp.concatenate([first, second], axis=0).astype(jnp.bfloat16)

    def contract(s):
        t = mate[s]
        col = lists[1, s]
        w = jnp.concatenate([weights(place[s], col), weights(place[t], col)], axis=0)
        a = jnp.concatenate([tiles[s], tiles[t]], axis=1)
        c = jnp.dot(a, w, preferred_element_type=jnp.float32).astype(jnp.bfloat16)
        out[s] = c
        return lax.dot_general(c, c, (((0,), (0,)), ((), ())), preferred_element_type=jnp.float32)

    def store_out(who, index):
        span = pl.ds(who * per_dev, per_dev)
        return pltpu.make_async_copy(out.at[span], out_hbm.at[span], out_sem.at[index])

    def send_pol(index, who, device):
        return pltpu.make_async_remote_copy(
            pol_send.at[who],
            pol_got.at[index],
            pol_out_sem.at[index],
            pol_in_sem.at[index],
            device,
            MESH,
        )

    routes = (
        (((1 - occ) * 2 + 1 - rep), other_both),
        (((1 - occ) * 2 + rep), other_x),
        ((occ * 2 + 1 - rep), other_core),
        (me, None),
    )
    for index, (who, device) in enumerate(routes):
        def pack(m, carry, who=who):
            s = who * per_dev + 2 * m
            g0 = contract(s)
            g1 = contract(s + 1)
            u = jnp.where(low, g0[:BLK], g1[BLK:])
            v = jnp.where(low, g1[:BLK], g0[BLK:])
            pol_send[who, m] = (u + pltpu.roll(v, BLK, 1)).astype(jnp.bfloat16)
            return carry

        lax.fori_loop(0, packs, pack, 0)
        if device is not None:
            send_pol(index, who, device).start()
        store_out(who, index).start()

    for index, (who, device) in enumerate(routes[:-1]):
        send_pol(index, who, device).wait()
    for m in range(packs):
        total = pol_send[me, m].astype(jnp.float32)
        for index in range(plane - 1):
            total = total + pol_got[index, m].astype(jnp.float32)
        spread[m * BLK : (m + 1) * BLK, :] = total
    even = spread[pl.ds(0, packs * BLK // 2, stride=2), :]
    odd = spread[pl.ds(1, packs * BLK // 2, stride=2), :]
    half = lax.broadcasted_iota(jnp.int32, even.shape, 1) < BLK
    first = jnp.where(half, even, pltpu.roll(odd, BLK, 1))
    second = jnp.where(half, pltpu.roll(even, BLK, 1), odd)
    rows = BLK // 2
    for m in range(packs):
        pol_ref[(2 * m) * rows : (2 * m + 1) * rows, :] = first[m * rows : (m + 1) * rows]
        pol_ref[(2 * m + 1) * rows : (2 * m + 2) * rows, :] = second[m * rows : (m + 1) * rows]
    for index, (who, _) in enumerate(routes):
        store_out(who, index).wait()


def fused(pair_tiles, block_list, owner_blocks, coulomb_metric):
    slots, occ_rows, merged = pair_tiles.shape
    pairs = lax.axis_size("pair")
    n_occ = lax.axis_size("occ")
    plane = n_occ * lax.axis_size("rep")
    groups = merged // LANES
    tile_rows = occ_rows * groups
    per_dev = slots // plane
    width = coulomb_metric.shape[1]
    flat = (
        pair_tiles.reshape(slots, occ_rows, groups, LANES)
        .transpose(0, 2, 1, 3)
        .reshape(slots, tile_rows, LANES)
    )
    dma = pltpu.SemaphoreType.DMA
    out, pol = pl.pallas_call(
        functools.partial(fused_kernel, pairs, n_occ, slots),
        out_shape=(
            jax.ShapeDtypeStruct((slots, tile_rows, LANES), jnp.bfloat16),
            jax.ShapeDtypeStruct((per_dev * merged // LANES, LANES), jnp.float32),
        ),
        in_specs=[
            pl.BlockSpec(memory_space=pltpu.SMEM),
            pl.BlockSpec(memory_space=pltpu.SMEM),
            pl.BlockSpec(memory_space=pl.ANY),
            pl.BlockSpec(memory_space=pl.ANY),
        ],
        out_specs=(
            pl.BlockSpec(memory_space=pl.ANY),
            pl.BlockSpec(memory_space=pltpu.VMEM),
        ),
        scratch_shapes=[
            pltpu.VMEM((pairs, plane, PBD, width // LANES, BLK, LANES), jnp.bfloat16),
            pltpu.VMEM((slots, tile_rows, LANES), jnp.bfloat16),
            pltpu.VMEM((slots, tile_rows, LANES), jnp.bfloat16),
            pltpu.VMEM((plane, per_dev // 2, BLK, LANES), jnp.bfloat16),
            pltpu.VMEM((plane - 1, per_dev // 2, BLK, LANES), jnp.bfloat16),
            pltpu.VMEM((per_dev // 2 * BLK, LANES), jnp.float32),
            pltpu.SMEM((slots,), jnp.int32),
            pltpu.SMEM((slots,), jnp.int32),
            dma((PBD, width // LANES)),
            dma,
            dma((plane,)),
            dma((pairs,)),
            dma((pairs,)),
            dma((pairs,)),
            dma((pairs,)),
            dma((pairs,)),
            dma((pairs, n_occ)),
            dma((pairs, n_occ)),
            dma((plane - 1,)),
            dma((plane - 1,)),
        ],
        compiler_params=pltpu.CompilerParams(
            collective_id=0, has_side_effects=True, vmem_limit_bytes=32 << 20
        ),
    )(block_list.T, owner_blocks, flat, coulomb_metric)
    contracted = (
        out.reshape(slots, groups, occ_rows, LANES)
        .transpose(0, 2, 1, 3)
        .reshape(slots, occ_rows, merged)
    )
    return contracted, pol.reshape(per_dev, merged)


def per_device(pair_tiles, block_list, owner_blocks, coulomb_metric):
    pairs = lax.axis_size("pair")
    plane = lax.axis_size("occ") * lax.axis_size("rep")
    gathered = coulomb_metric.size * 2 * pairs * plane
    if gathered <= GATHER_LIMIT and lax.axis_size("occ") == 2 and lax.axis_size("rep") == 2:
        return fused(pair_tiles, block_list, owner_blocks, coulomb_metric)
    return block_exchange(pair_tiles, block_list, owner_blocks, coulomb_metric)


def solution(mesh):
    placed = (
        P(("grp", "pair"), ("occ", "rep"), None),
        P(("grp", "pair"), None),
        P("grp", None),
        P(("grp", "pair"), ("occ", "rep")),
    )
    return jax.shard_map(
        per_device,
        mesh=mesh,
        in_specs=placed,
        out_specs=(
            P(("grp", "pair"), ("occ", "rep"), None),
            P(("grp", "pair", "occ", "rep"), None),
        ),
        check_vma=False,
    )
```

time: 168 us -> 37.9 us (0.23)
  waiting for transfers between devices: 89.1 us -> 0 us
  Pallas kernels: 0 us -> 32.7 us
  local copies, waits for them, and re-layouts: 33.2 us -> 4.27 us
  starting transfers between devices: 19.1 us -> 0 us
  blocking collectives: 16.8 us -> 0 us
  other arithmetic: 4.58 us -> 0 us
  matrix products: 3.02 us -> 0 us
    all_to_all x3 -> x0, waiting for transfers between devices: 89.1 us -> none  [the longest x1 68.9 us: per_device(): lax.all_to_all(products, 'pair', split_axis=0, concat_axis=0, tiled=True)]
    pallas_call x0 -> x1, Pallas kernels: none -> 32.7 us  [fused(): pl.pallas_call(functools.partial(fused_kernel, pairs, n_occ, slots), out_...]
    all_to_all x3 -> x0, starting transfers between devices: 14.8 us -> none  [the longest x1 5.42 us: per_device(): lax.all_to_all(send_meta, 'pair', split_axis=0, concat_axis=0, tiled=True)]
    convert_element_type x5 -> x0, local copies, waits for them, and re-layouts: 9.88 us -> none  [the longest x2 5.22 us: per_device(): own_products[partner_index, 1].astype(jnp.float32)]
    all_gather x1 -> x0, blocking collectives: 8.51 us -> none  [per_device(): strip = lax.all_gather(coulomb_metric, ('occ', 'rep'), axis=1, tiled=True)]
    unnamed x1 -> x0, blocking collectives: 8.33 us -> none
    gather x6 -> x0, local copies, waits for them, and re-layouts: 7.7 us -> none  [the longest x2 3.26 us: pick_blocks(): other_block = strip_blocks[block_meta[:, 0], block_meta[:, 2]]]
    reshape x4 -> x1, local copies, waits for them, and re-layouts: 6.46 us -> 0.67 us  [fused(): return (contracted, pol.reshape(per_dev, merged))]
  transfers between devices with their start and end apart: 4 -> 0, of which waited for: 2 -> 0; matrix products, arithmetic and copies ran while one was open for 16% -> 0% of each run, Pallas kernels for 0% -> 0%
where the time goes in v1:
time: 37.9 us; the launch traced here: 37.6 us
  Pallas kernels  32.7 us (86%)
  local copies, waits for them, and re-layouts  4.27 us (11%)
  between operations  0.66 us (2%)
    pallas_call x1, Pallas kernels, fused(): pl.pallas_call(functools.partial(fused_kernel, pairs, n_occ, slots), out_...  32.7 us
    unnamed x9, local copies, waits for them, and re-layouts  3.59 us

profile of v1, /device:TPU:1, one launch (start us, length us, event | category | flops | bytes accessed | tf_op | source)
XLA Modules:
  0.0 37.6 jit_solution(11172558140559569935)
XLA Ops:
  0.6 0.0 copy-start.2
  0.6 0.0 copy-start.3
  0.7 0.7 %copy-done.2 = s32[4,4]{1,0:T(4,128)S(1)} copy-done((s32[4,4]{1,0:T(4,128)S(1)}, s32[4,4]{1,0:T(4,128)}, u32[]{:S(2)}) %copy-start.2) | copy-done | bytes 88
  1.3 0.0 copy-done.3
  1.3 0.0 copy-start
  1.3 1.1 %copy-done = bf16[24,4,4096]{2,1,0:T(4,128)(2,1)S(1)} copy-done((bf16[24,4,4096]{2,1,0:T(4,128)(2,1)S(1)}, bf16[24,4,4096]{2,1,0:T(4,128)(2,1)}, u32[]{:S(2)}) %copy-start) | copy-done | bytes 786456
  2.5 0.0 copy-start.1
  2.5 0.9 %copy-done.1 = bf16[256,256]{1,0:T(8,128)(2,1)S(1)} copy-done((bf16[256,256]{1,0:T(8,128)(2,1)S(1)}, bf16[256,256]{1,0:T(8,128)(2,1)}, u32[]{:S(2)}) %copy-start.1) | copy-done | bytes 131096
  3.4 32.7 %shard_map.59 = (bf16[24,128,128]{2,1,0:T(8,128)(2,1)S(1)}, f32[192,128]{1,0:T(8,128)S(1)}) custom-call(s32[2,24]{1,0:T(2,128)S(1)} %bitcast.13, s32[4,4]{1,0:T(4,128)S(1)} %copy-done.2, bf16[24,128,128]{2,1,0:T(8,128)(2,1)S(1)} %bitcast.12, bf16[256,256]{1,0:T(8,128)(2,1)S(1)} %copy-done.1), custom_call_target="tpu_custom_call" | custom-call | tf_op jit(solution)/shard_map/pallas_call | solution.py:373
  36.1 0.7 %reshape.23 = f32[6,4096]{1,0:T(8,128)} reshape(f32[192,128]{1,0:T(8,128)S(1)} %get-tuple-element.5) | data formatting | bytes 196608 | tf_op jit(solution)/shard_map/reshape | solution.py:420
  36.7 0.9 %copy.9 = bf16[24,4,4096]{2,1,0:T(4,128)(2,1)} copy(bf16[24,4,4096]{2,1,0:T(4,128)(2,1)S(1)} %bitcast.11) | data formatting | bytes 1572864
Async XLA Ops:
  0.6 0.7 %copy-start.2 = (s32[4,4]{1,0:T(4,128)S(1)}, s32[4,4]{1,0:T(4,128)}, u32[]{:S(2)}) copy-start(s32[4,4]{1,0:T(4,128)} %owners.1) | copy-start | bytes 196
  0.6 0.7 %copy-start.3 = (s32[24,2]{0,1:T(2,128)S(1)}, s32[24,2]{0,1:T(2,128)}, u32[]{:S(2)}) copy-start(s32[24,2]{0,1:T(2,128)} %param.5) | copy-start | bytes 580
  1.3 1.1 %copy-start = (bf16[24,4,4096]{2,1,0:T(4,128)(2,1)S(1)}, bf16[24,4,4096]{2,1,0:T(4,128)(2,1)}, u32[]{:S(2)}) copy-start(bf16[24,4,4096]{2,1,0:T(4,128)(2,1)} %param.4) | copy-start | bytes 2359300
  2.5 0.9 %copy-start.1 = (bf16[256,256]{1,0:T(8,128)(2,1)S(1)}, bf16[256,256]{1,0:T(8,128)(2,1)}, u32[]{:S(2)}) copy-start(bf16[256,256]{1,0:T(8,128)(2,1)} %metric_hbm.1) | copy-start | bytes 393220

commit v2 on v1

--- a/solution.py
+++ b/solution.py
@@ -12,6 +12,7 @@
 LANES = 128
 MESH = pl.DeviceIdType.MESH
 GATHER_LIMIT = 8 << 20
+CHUNKS = 2
 
 
 def block_exchange(pair_tiles, block_list, owner_blocks, coulomb_metric):
@@ -61,8 +62,8 @@
     pairs,
     n_occ,
     slots,
-    lists,
-    owners,
+    lists_hbm,
+    owners_hbm,
     tiles_hbm,
     metric_hbm,
     out_hbm,
@@ -73,10 +74,13 @@
     pol_send,
     pol_got,
     spread,
+    lists,
+    owners,
     place,
     mate,
     local_sem,
     tiles_sem,
+    table_sem,
     out_sem,
     right_send,
     left_send,
@@ -93,7 +97,8 @@
     rep = lax.axis_index("rep")
     plane = 2 * n_occ
     me = occ * 2 + rep
-    halves = held.shape[3]
+    halves = held.shape[4]
+    part = PBD // CHUNKS
     per_dev = slots // plane
     packs = per_dev // 2
     other_x = {"occ": 1 - occ}
@@ -103,7 +108,7 @@
     load_metric = [
         pltpu.make_async_copy(
             metric_hbm.at[k * BLK : (k + 1) * BLK, h * LANES : (h + 1) * LANES],
-            held.at[j, me, k, h],
+            held.at[j, occ, rep, k, h],
             local_sem.at[k, h],
         )
         for k in range(PBD)
@@ -113,6 +118,10 @@
         copy.start()
     load_tiles = pltpu.make_async_copy(tiles_hbm, tiles, tiles_sem)
     load_tiles.start()
+    load_lists = pltpu.make_async_copy(lists_hbm, lists, table_sem.at[0])
+    load_lists.start()
+    load_owners = pltpu.make_async_copy(owners_hbm, owners, table_sem.at[1])
+    load_owners.start()
 
     barrier = pltpu.get_barrier_semaphore()
 
@@ -141,62 +150,45 @@
     def _():
         pl.semaphore_wait(barrier, 4)
 
-    for copy in load_metric:
-        copy.wait()
-
-    def right(o):
+
+    def chunk(o, x, core, k):
+        return held.at[o, x, core, pl.ds(k * part, part)]
+
+    def right(o, k):
+        c = chunk(o, occ, rep, k)
         return pltpu.make_async_remote_copy(
-            held.at[o, me], held.at[o, me], right_send.at[o], line_got.at[o], {"pair": j + 1}, MESH
+            c, c, right_send.at[o], line_got.at[o, k], {"pair": j + 1}, MESH
         )
 
-    def left(o):
+    def left(o, k):
+        c = chunk(o, occ, rep, k)
         return pltpu.make_async_remote_copy(
-            held.at[o, me], held.at[o, me], left_send.at[o], line_got.at[o], {"pair": j - 1}, MESH
+            c, c, left_send.at[o], line_got.at[o, k], {"pair": j - 1}, MESH
         )
 
-    def across(o):
-        return pltpu.make_async_remote_copy(
-            held.at[o, me], held.at[o, me], x_send.at[o], x_got.at[o], other_x, MESH
-        )
-
-    def arrived_x(o):
-        col = (1 - occ) * 2 + rep
-        return pltpu.make_async_remote_copy(
-            held.at[o, col], held.at[o, col], x_send.at[o], x_got.at[o], other_x, MESH
-        )
-
-    def to_core(o, which):
-        col = which * 2 + rep
-        return pltpu.make_async_remote_copy(
-            held.at[o, col],
-            held.at[o, col],
-            core_send.at[o, which],
-            core_got.at[o, which],
-            other_core,
-            MESH,
-        )
-
-    def from_core(o, which):
-        col = which * 2 + 1 - rep
-        return pltpu.make_async_remote_copy(
-            held.at[o, col],
-            held.at[o, col],
-            core_send.at[o, which],
-            core_got.at[o, which],
-            other_core,
-            MESH,
-        )
-
-    @pl.when(j < pairs - 1)
-    def _():
-        right(j).start()
-
-    @pl.when(j > 0)
-    def _():
-        left(j).start()
-
-    across(j).start()
-    to_core(j, occ).start()
+    def across(o, k, x=occ):
+        c = chunk(o, x, rep, k)
+        return pltpu.make_async_remote_copy(c, c, x_send, x_got.at[o, k], other_x, MESH)
+
+    def to_core(o, x, k):
+        c = chunk(o, x, rep, k)
+        return pltpu.make_async_remote_copy(c, c, core_send, core_got, other_core, MESH)
+
+    for k in range(CHUNKS):
+        for copy in load_metric[k * part * halves : (k + 1) * part * halves]:
+            copy.wait()
+
+        @pl.when(j < pairs - 1)
+        def _(k=k):
+            right(j, k).start()
+
+        @pl.when(j > 0)
+        def _(k=k):
+            left(j, k).start()
+
+        across(j, k).start()
+    for k in range(CHUNKS):
+        to_core(j, occ, k).start()
 
     def find(s, carry):
         aux = lists[1, s]
@@ -211,80 +203,62 @@
         mate[s] = other
         return carry
 
+    load_lists.wait()
+    load_owners.wait()
     lax.fori_loop(0, slots, find, 0)
 
-    def from_x(o):
-        arrived_x(o).wait_recv()
-        to_core(o, 1 - occ).start()
-
-    from_x_levels = [[j]]
-    for d in range(1, pairs):
-        lo, hi = j - d, j + d
-
-        @pl.when(lo >= 0)
-        def _(lo=lo):
-            right(lo).wait_recv()
-
-            @pl.when(j < pairs - 1)
-            def _():
-                right(lo).start()
-
-            across(lo).start()
-            to_core(lo, occ).start()
-
-        @pl.when(hi < pairs)
-        def _(hi=hi):
-            left(hi).wait_recv()
-
-            @pl.when(j > 0)
-            def _():
-                left(hi).start()
-
-            across(hi).start()
-            to_core(hi, occ).start()
-
-        if d == 1:
-            from_x(j)
-        else:
-            for o in (j - d + 1, j + d - 1):
-
-                @pl.when((o >= 0) & (o < pairs))
-                def _(o=o):
-                    from_x(o)
-
-    for o in (j - pairs + 1, j + pairs - 1):
-
-        @pl.when((o >= 0) & (o < pairs))
-        def _(o=o):
-            from_x(o)
+    def from_x(o, k):
+        across(o, k, 1 - occ).wait_recv()
+        to_core(o, 1 - occ, k).start()
+
+    for d in range(1, pairs + 1):
+        for k in range(CHUNKS):
+            if d < pairs:
+                lo, hi = j - d, j + d
+
+                @pl.when(lo >= 0)
+                def _(lo=lo, k=k):
+                    right(lo, k).wait_recv()
+
+                    @pl.when(j < pairs - 1)
+                    def _():
+                        right(lo, k).start()
+
+                    across(lo, k).start()
+                    to_core(lo, occ, k).start()
+
+                @pl.when(hi < pairs)
+                def _(hi=hi, k=k):
+                    left(hi, k).wait_recv()
+
+                    @pl.when(j > 0)
+                    def _():
+                        left(hi, k).start()
+
+                    across(hi, k).start()
+                    to_core(hi, occ, k).start()
+
+            if d == 1:
+                from_x(j, k)
+            else:
+                for o in (j - d + 1, j + d - 1):
+
+                    @pl.when((o >= 0) & (o < pairs))
+                    def _(o=o, k=k):
+                        from_x(o, k)
 
     load_tiles.wait()
 
-    def settle(o, carry):
-        from_core(o, 0).wait_recv()
-        from_core(o, 1).wait_recv()
-        to_core(o, 0).wait_send()
-        to_core(o, 1).wait_send()
-        across(o).wait_send()
-
-        @pl.when((o <= j) & (j < pairs - 1))
-        def _():
-            right(o).wait_send()
-
-        @pl.when((o >= j) & (j > 0))
-        def _():
-            left(o).wait_send()
-
-        return carry
-
-    lax.fori_loop(0, pairs, settle, 0)
+    theirs = held.at[:, :, 1 - rep]
+    pltpu.make_async_remote_copy(theirs, theirs, core_send, core_got, other_core, MESH).wait_recv()
 
     lane = lax.broadcasted_iota(jnp.int32, (BLK, LANES), 1)
     low = lane < BLK
 
     def weights(row, col):
         half = col // 2
-        x = held[row // PBD, half // halves, row % PBD, half % halves].astype(jnp.float32)
+        dev = half // halves
+        x = held[row // PBD, dev // 2, dev % 2, row % PBD, half % halves].astype(jnp.float32)
         turned = pltpu.roll(x, BLK, 1)
         even = jnp.full((BLK, LANES), col % 2, jnp.int32) == 0
         first = jnp.where(low, jnp.where(even, x, turned), 0.0)
@@ -353,6 +327,30 @@
         pol_ref[(2 * m + 1) * rows : (2 * m + 2) * rows, :] = second[m * rows : (m + 1) * rows]
     for index, (who, _) in enumerate(routes):
         store_out(who, index).wait()
+
+    mine = held.at[:, :, rep]
+    pltpu.make_async_remote_copy(mine, mine, core_send, core_got, other_core, MESH).wait_send()
+    column = held.at[:, occ, rep]
+    pltpu.make_async_remote_copy(column, column, x_send, x_got.at[0, 0], other_x, MESH).wait_send()
+
+    def settle(o, carry):
+        block = held.at[o, occ, rep]
+
+        @pl.when((o <= j) & (j < pairs - 1))
+        def _():
+            pltpu.make_async_remote_copy(
+                block, block, right_send.at[o], line_got.at[o, 0], {"pair": j + 1}, MESH
+            ).wait_send()
+
+        @pl.when((o >= j) & (j > 0))
+        def _():
+            pltpu.make_async_remote_copy(
+                block, block, left_send.at[o], line_got.at[o, 0], {"pair": j - 1}, MESH
+            ).wait_send()
+
+        return carry
+
+    lax.fori_loop(0, pairs, settle, 0)
 
 
 def fused(pair_tiles, block_list, owner_blocks, coulomb_metric):
@@ -377,34 +375,37 @@
             jax.ShapeDtypeStruct((per_dev * merged // LANES, LANES), jnp.float32),
         ),
         in_specs=[
-            pl.BlockSpec(memory_space=pltpu.SMEM),
-            pl.BlockSpec(memory_space=pltpu.SMEM),
-            pl.BlockSpec(memory_space=pl.ANY),
-            pl.BlockSpec(memory_space=pl.ANY),
+            pl.BlockSpec(memory_space=pltpu.HBM),
+            pl.BlockSpec(memory_space=pltpu.HBM),
+            pl.BlockSpec(memory_space=pltpu.HBM),
+            pl.BlockSpec(memory_space=pltpu.HBM),
         ],
         out_specs=(
             pl.BlockSpec(memory_space=pl.ANY),
             pl.BlockSpec(memory_space=pltpu.VMEM),
         ),
         scratch_shapes=[
-            pltpu.VMEM((pairs, plane, PBD, width // LANES, BLK, LANES), jnp.bfloat16),
+            pltpu.VMEM((pairs, n_occ, 2, PBD, width // LANES, BLK, LANES), jnp.bfloat16),
             pltpu.VMEM((slots, tile_rows, LANES), jnp.bfloat16),
             pltpu.VMEM((slots, tile_rows, LANES), jnp.bfloat16),
             pltpu.VMEM((plane, per_dev // 2, BLK, LANES), jnp.bfloat16),
             pltpu.VMEM((plane - 1, per_dev // 2, BLK, LANES), jnp.bfloat16),
             pltpu.VMEM((per_dev // 2 * BLK, LANES), jnp.float32),
+            pltpu.SMEM((2, slots), jnp.int32),
+            pltpu.SMEM(owner_blocks.shape, jnp.int32),
             pltpu.SMEM((slots,), jnp.int32),
             pltpu.SMEM((slots,), jnp.int32),
             dma((PBD, width // LANES)),
             dma,
+            dma((2,)),
             dma((plane,)),
             dma((pairs,)),
             dma((pairs,)),
-            dma((pairs,)),
-            dma((pairs,)),
-            dma((pairs,)),
-            dma((pairs, n_occ)),
-            dma((pairs, n_occ)),
+            dma((pairs, CHUNKS)),
+            dma,
+            dma((pairs, CHUNKS)),
+            dma,
+            dma,
             dma((plane - 1,)),
             dma((plane - 1,)),
         ],

time: 37.9 us -> 35 us (0.923)
  Pallas kernels: 32.7 us -> 29.9 us
    pallas_call x1, Pallas kernels: 32.7 us -> 29.9 us  [fused(): pl.pallas_call(functools.partial(fused_kernel, pairs, n_occ, slots), out_...]
where the time goes in v2:
time: 35 us; the launch traced here: 34.8 us
  Pallas kernels  29.9 us (85%)
  local copies, waits for them, and re-layouts  4.27 us (12%)
  between operations  0.66 us (2%)
    pallas_call x1, Pallas kernels, fused(): pl.pallas_call(functools.partial(fused_kernel, pairs, n_occ, slots), out_...  29.9 us
    unnamed x9, local copies, waits for them, and re-layouts  3.59 us

profile of v2, /device:TPU:1, one launch (start us, length us, event | category | flops | bytes accessed | tf_op | source)
XLA Modules:
  0.0 34.8 jit_solution(12020812529667714713)
XLA Ops:
  0.6 0.0 copy-start.2
  0.6 0.0 copy-start.3
  0.7 0.7 %copy-done.2 = s32[4,4]{1,0:T(4,128)S(1)} copy-done((s32[4,4]{1,0:T(4,128)S(1)}, s32[4,4]{1,0:T(4,128)}, u32[]{:S(2)}) %copy-start.2) | copy-done | bytes 88
  1.3 0.0 copy-done.3
  1.3 0.0 copy-start
  1.3 1.1 %copy-done = bf16[24,4,4096]{2,1,0:T(4,128)(2,1)S(1)} copy-done((bf16[24,4,4096]{2,1,0:T(4,128)(2,1)S(1)}, bf16[24,4,4096]{2,1,0:T(4,128)(2,1)}, u32[]{:S(2)}) %copy-start) | copy-done | bytes 786456
  2.5 0.0 copy-start.1
  2.5 0.9 %copy-done.1 = bf16[256,256]{1,0:T(8,128)(2,1)S(1)} copy-done((bf16[256,256]{1,0:T(8,128)(2,1)S(1)}, bf16[256,256]{1,0:T(8,128)(2,1)}, u32[]{:S(2)}) %copy-start.1) | copy-done | bytes 131096
  3.4 29.9 %shard_map.59 = (bf16[24,128,128]{2,1,0:T(8,128)(2,1)S(1)}, f32[192,128]{1,0:T(8,128)S(1)}) custom-call(s32[2,24]{1,0:T(2,128)S(1)} %bitcast.13, s32[4,4]{1,0:T(4,128)S(1)} %copy-done.2, bf16[24,128,128]{2,1,0:T(8,128)(2,1)S(1)} %bitcast.12, bf16[256,256]{1,0:T(8,128)(2,1)S(1)} %copy-done.1), custom_call_target="tpu_custom_call" | custom-call | tf_op jit(solution)/shard_map/pallas_call | solution.py:371
  33.3 0.7 %reshape.23 = f32[6,4096]{1,0:T(8,128)} reshape(f32[192,128]{1,0:T(8,128)S(1)} %get-tuple-element.5) | data formatting | bytes 196608 | tf_op jit(solution)/shard_map/reshape | solution.py:421
  33.9 0.9 %copy.9 = bf16[24,4,4096]{2,1,0:T(4,128)(2,1)} copy(bf16[24,4,4096]{2,1,0:T(4,128)(2,1)S(1)} %bitcast.11) | data formatting | bytes 1572864
Async XLA Ops:
  0.6 0.7 %copy-start.2 = (s32[4,4]{1,0:T(4,128)S(1)}, s32[4,4]{1,0:T(4,128)}, u32[]{:S(2)}) copy-start(s32[4,4]{1,0:T(4,128)} %owners_hbm.1) | copy-start | bytes 196
  0.6 0.7 %copy-start.3 = (s32[24,2]{0,1:T(2,128)S(1)}, s32[24,2]{0,1:T(2,128)}, u32[]{:S(2)}) copy-start(s32[24,2]{0,1:T(2,128)} %param.5) | copy-start | bytes 580
  1.3 1.1 %copy-start = (bf16[24,4,4096]{2,1,0:T(4,128)(2,1)S(1)}, bf16[24,4,4096]{2,1,0:T(4,128)(2,1)}, u32[]{:S(2)}) copy-start(bf16[24,4,4096]{2,1,0:T(4,128)(2,1)} %param.4) | copy-start | bytes 2359300
  2.5 0.9 %copy-start.1 = (bf16[256,256]{1,0:T(8,128)(2,1)S(1)}, bf16[256,256]{1,0:T(8,128)(2,1)}, u32[]{:S(2)}) copy-start(bf16[256,256]{1,0:T(8,128)(2,1)} %metric_hbm.1) | copy-start | bytes 393220

commit v3 on v2

--- a/solution.py
+++ b/solution.py
@@ -304,7 +304,7 @@
             pol_send[who, m] = (u + pltpu.roll(v, BLK, 1)).astype(jnp.bfloat16)
             return carry
 
-        lax.fori_loop(0, packs, pack, 0)
+        lax.fori_loop(0, packs, pack, 0, unroll=True)
         if device is not None:
             send_pol(index, who, device).start()
         store_out(who, index).start()

time: 35 us -> 32.9 us (0.940)
  Pallas kernels: 29.9 us -> 27.8 us
    pallas_call x1, Pallas kernels: 29.9 us -> 27.8 us  [fused(): pl.pallas_call(functools.partial(fused_kernel, pairs, n_occ, slots), out_...]
where the time goes in v3:
time: 32.9 us; the launch traced here: 32.7 us
  Pallas kernels  27.8 us (84%)
  local copies, waits for them, and re-layouts  4.27 us (13%)
  between operations  0.66 us (2%)
    pallas_call x1, Pallas kernels, fused(): pl.pallas_call(functools.partial(fused_kernel, pairs, n_occ, slots), out_...  27.8 us
    unnamed x9, local copies, waits for them, and re-layouts  3.59 us
    reshape x1, local copies, waits for them, and re-layouts, fused(): return (contracted, pol.reshape(per_dev, merged))  0.67 us

profile of v3, /device:TPU:1, one launch (start us, length us, event | category | flops | bytes accessed | tf_op | source)
XLA Modules:
  0.0 32.7 jit_solution(14919845065688565477)
XLA Ops:
  0.6 0.0 copy-start.2
  0.6 0.0 copy-start.3
  0.7 0.7 %copy-done.2 = s32[4,4]{1,0:T(4,128)S(1)} copy-done((s32[4,4]{1,0:T(4,128)S(1)}, s32[4,4]{1,0:T(4,128)}, u32[]{:S(2)}) %copy-start.2) | copy-done | bytes 88
  1.3 0.0 copy-done.3
  1.3 0.0 copy-start
  1.3 1.1 %copy-done = bf16[24,4,4096]{2,1,0:T(4,128)(2,1)S(1)} copy-done((bf16[24,4,4096]{2,1,0:T(4,128)(2,1)S(1)}, bf16[24,4,4096]{2,1,0:T(4,128)(2,1)}, u32[]{:S(2)}) %copy-start) | copy-done | bytes 786456
  2.5 0.0 copy-start.1
  2.5 0.9 %copy-done.1 = bf16[256,256]{1,0:T(8,128)(2,1)S(1)} copy-done((bf16[256,256]{1,0:T(8,128)(2,1)S(1)}, bf16[256,256]{1,0:T(8,128)(2,1)}, u32[]{:S(2)}) %copy-start.1) | copy-done | bytes 131096
  3.4 27.8 %shard_map.59 = (bf16[24,128,128]{2,1,0:T(8,128)(2,1)S(1)}, f32[192,128]{1,0:T(8,128)S(1)}) custom-call(s32[2,24]{1,0:T(2,128)S(1)} %bitcast.13, s32[4,4]{1,0:T(4,128)S(1)} %copy-done.2, bf16[24,128,128]{2,1,0:T(8,128)(2,1)S(1)} %bitcast.12, bf16[256,256]{1,0:T(8,128)(2,1)S(1)} %copy-done.1), custom_call_target="tpu_custom_call" | custom-call | tf_op jit(solution)/shard_map/pallas_call | solution.py:371
  31.1 0.7 %reshape.23 = f32[6,4096]{1,0:T(8,128)} reshape(f32[192,128]{1,0:T(8,128)S(1)} %get-tuple-element.5) | data formatting | bytes 196608 | tf_op jit(solution)/shard_map/reshape | solution.py:421
  31.8 0.9 %copy.9 = bf16[24,4,4096]{2,1,0:T(4,128)(2,1)} copy(bf16[24,4,4096]{2,1,0:T(4,128)(2,1)S(1)} %bitcast.11) | data formatting | bytes 1572864
Async XLA Ops:
  0.6 0.7 %copy-start.2 = (s32[4,4]{1,0:T(4,128)S(1)}, s32[4,4]{1,0:T(4,128)}, u32[]{:S(2)}) copy-start(s32[4,4]{1,0:T(4,128)} %owners_hbm.1) | copy-start | bytes 196
  0.6 0.7 %copy-start.3 = (s32[24,2]{0,1:T(2,128)S(1)}, s32[24,2]{0,1:T(2,128)}, u32[]{:S(2)}) copy-start(s32[24,2]{0,1:T(2,128)} %param.5) | copy-start | bytes 580
  1.3 1.1 %copy-start = (bf16[24,4,4096]{2,1,0:T(4,128)(2,1)S(1)}, bf16[24,4,4096]{2,1,0:T(4,128)(2,1)}, u32[]{:S(2)}) copy-start(bf16[24,4,4096]{2,1,0:T(4,128)(2,1)} %param.4) | copy-start | bytes 2359300
  2.5 0.9 %copy-start.1 = (bf16[256,256]{1,0:T(8,128)(2,1)S(1)}, bf16[256,256]{1,0:T(8,128)(2,1)}, u32[]{:S(2)}) copy-start(bf16[256,256]{1,0:T(8,128)(2,1)} %metric_hbm.1) | copy-start | bytes 393220

commit v4 on v3

--- a/solution.py
+++ b/solution.py
@@ -410,7 +410,7 @@
             dma((plane - 1,)),
         ],
         compiler_params=pltpu.CompilerParams(
-            collective_id=0, has_side_effects=True, vmem_limit_bytes=32 << 20
+            collective_id=0, has_side_effects=True, vmem_limit_bytes=105 << 19
         ),
     )(block_list.T, owner_blocks, flat, coulomb_metric)
     contracted = (

time: 32.9 us -> 31.7 us (0.964)
  local copies, waits for them, and re-layouts: 4.27 us -> 3.13 us
    unnamed x9 -> x7, local copies, waits for them, and re-layouts: 3.59 us -> 2.46 us
where the time goes in v4:
time: 31.7 us; the launch traced here: 31.5 us
  Pallas kernels  27.7 us (87%)
  local copies, waits for them, and re-layouts  3.13 us (10%)
  between operations  0.66 us (2%)
    pallas_call x1, Pallas kernels, fused(): pl.pallas_call(functools.partial(fused_kernel, pairs, n_occ, slots), out_...  27.7 us
    unnamed x7, local copies, waits for them, and re-layouts  2.46 us
    reshape x1, local copies, waits for them, and re-layouts, fused(): return (contracted, pol.reshape(per_dev, merged))  0.67 us

profile of v4, /device:TPU:1, one launch (start us, length us, event | category | flops | bytes accessed | tf_op | source)
XLA Modules:
  0.0 31.5 jit_solution(4015696207621156641)
XLA Ops:
  0.6 0.0 copy-start.1
  0.6 0.0 copy-start.2
  0.7 0.7 %copy-done.1 = s32[4,4]{1,0:T(4,128)S(1)} copy-done((s32[4,4]{1,0:T(4,128)S(1)}, s32[4,4]{1,0:T(4,128)}, u32[]{:S(2)}) %copy-start.1) | copy-done | bytes 88
  1.3 0.0 copy-done.2
  1.3 0.0 copy-start
  1.3 0.9 %copy-done = bf16[256,256]{1,0:T(8,128)(2,1)S(1)} copy-done((bf16[256,256]{1,0:T(8,128)(2,1)S(1)}, bf16[256,256]{1,0:T(8,128)(2,1)}, u32[]{:S(2)}) %copy-start) | copy-done | bytes 131096
  2.2 27.7 %shard_map.59 = (bf16[24,128,128]{2,1,0:T(8,128)(2,1)S(1)}, f32[192,128]{1,0:T(8,128)S(1)}) custom-call(s32[2,24]{1,0:T(2,128)S(1)} %bitcast.12, s32[4,4]{1,0:T(4,128)S(1)} %copy-done.1, bf16[24,128,128]{2,1,0:T(8,128)(2,1)} %bitcast.13, bf16[256,256]{1,0:T(8,128)(2,1)S(1)} %copy-done), custom_call_target="tpu_custom_call" | custom-call | tf_op jit(solution)/shard_map/pallas_call | solution.py:371
  30.0 0.7 %reshape.23 = f32[6,4096]{1,0:T(8,128)} reshape(f32[192,128]{1,0:T(8,128)S(1)} %get-tuple-element.5) | data formatting | bytes 196608 | tf_op jit(solution)/shard_map/reshape | solution.py:421
  30.6 0.9 %copy.9 = bf16[24,4,4096]{2,1,0:T(4,128)(2,1)} copy(bf16[24,4,4096]{2,1,0:T(4,128)(2,1)S(1)} %bitcast.11) | data formatting | bytes 1572864
Async XLA Ops:
  0.6 0.7 %copy-start.1 = (s32[4,4]{1,0:T(4,128)S(1)}, s32[4,4]{1,0:T(4,128)}, u32[]{:S(2)}) copy-start(s32[4,4]{1,0:T(4,128)} %owners_hbm.1) | copy-start | bytes 196
  0.6 0.7 %copy-start.2 = (s32[24,2]{0,1:T(2,128)S(1)}, s32[24,2]{0,1:T(2,128)}, u32[]{:S(2)}) copy-start(s32[24,2]{0,1:T(2,128)} %param.5) | copy-start | bytes 580
  1.3 0.9 %copy-start = (bf16[256,256]{1,0:T(8,128)(2,1)S(1)}, bf16[256,256]{1,0:T(8,128)(2,1)}, u32[]{:S(2)}) copy-start(bf16[256,256]{1,0:T(8,128)(2,1)} %metric_hbm.1) | copy-start | bytes 393220
